TPU v7x, 32 devices: a whole 2x2x4 slice. The times are simulated.
32 devices in a mesh: expert: 4 (over z), tensor: 8 (over y, x, core).
Axes of the slice: x: 2, y: 2, z: 4, core: 2. Of those that a mesh axis runs over, the one named last changes fastest.
Arguments:
- activations: bfloat16 [3072, 512], P('tensor', 'expert'), may hold values from -6 to 6
- cotangent: bfloat16 [3072, 512], P('tensor', 'expert'), may hold values from -4 to 4
- route_ids: int32 [512, 2], P('expert'), may hold values from 0 to 3, all different within a row; in each aligned block of 128 rows (0 to 127, 128 to 255, ...) at most 80 rows name the same one
- gate_probs: float32 [512, 2], P('expert'), may hold values from 0.2 to 0.8
- gate_weight: bfloat16 [4, 3072, 16384], P('expert', None, 'tensor'), may hold values from -0.15625 to 0.15625
- up_weight: bfloat16 [4, 3072, 16384], P('expert', None, 'tensor'), may hold values from -0.15625 to 0.15625
- down_weight: bfloat16 [4, 16384, 3072], P('expert', 'tensor'), may hold values from -0.046875 to 0.046875
Outputs:
- grad_input: bfloat16 [3072, 512], P('tensor', 'expert')
- score_grad: float32 [512, 2], P('expert')
Inputs may be any that keep to these rules, and one draw needn't show every extreme that they name: `route_ids`: each token names 2 different experts. Among the 128 tokens of one index of the expert axis no expert is named more than 80 times, and in every draw some such block names one expert exactly 80 times.
All inputs are finite; a program needn't handle non-finite values.
Results may differ from a plain program's by a relative error of at most 0.008.
Values may be sent and summed in bfloat16 or wider, within the bound.
A program may use at most 128 MiB of HBM per device.

v0:
```python
import jax
import jax.numpy as jnp
from jax import lax
from jax.sharding import PartitionSpec as P

EXTRA_ROWS = 16


def slot_numbers(route_ids, expert_count, capacity):
    token_count = route_ids.shape[0]
    onehot = route_ids[:, :, None] == jnp.arange(expert_count, dtype=jnp.int32)[None, None, :]
    named = jnp.sum(onehot.astype(jnp.float32), axis=1).astype(jnp.bfloat16)
    order = jnp.arange(token_count, dtype=jnp.int32)
    before = (order[None, :] < order[:, None]).astype(jnp.bfloat16)
    earlier = jnp.dot(before, named, preferred_element_type=jnp.float32)
    position = jnp.sum(jnp.where(onehot, earlier[:, None, :], 0.0), axis=2).astype(jnp.int32)
    return route_ids * capacity + position


def swiglu_backward(gate_sum, up_sum, hidden_grad):
    sigma = jax.nn.sigmoid(gate_sum)
    silu_value = gate_sum * sigma
    grad_up = (hidden_grad * silu_value).astype(jnp.bfloat16)
    grad_gate = (hidden_grad * up_sum * sigma * (1.0 + gate_sum * (1.0 - sigma))).astype(
        jnp.bfloat16
    )
    score_rows = jnp.sum(silu_value * up_sum * hidden_grad, axis=1)
    return (grad_gate, grad_up, score_rows)


def body(activations, cotangent, route_ids, gate_probs, gate_weight, up_weight, down_weight):
    expert_count = lax.axis_size("expert")
    tokens_here = route_ids.shape[0]
    capacity = min(tokens_here, 5 * tokens_here // (2 * expert_count))
    slot_total = expert_count * capacity
    destination = slot_numbers(route_ids, expert_count, capacity)
    slot_range = jnp.arange(slot_total, dtype=jnp.int32)
    matches = destination[:, :, None] == slot_range[None, None, :]
    placing = jnp.sum(matches.astype(jnp.float32), axis=1).astype(jnp.bfloat16)
    weighting = jnp.sum(jnp.where(matches, gate_probs[:, :, None], jnp.float32(0.0)), axis=1)
    gate_local = gate_weight[0]
    up_local = up_weight[0]
    down_local = down_weight[0]
    first_dims = (((0,), (0,)), ((), ()))
    down_dims = (((0,), (1,)), ((), ()))
    hidden_dims = (((1,), (1,)), ((), ()))
    features_here = activations.shape[0]
    send_in = jnp.dot(activations, placing, preferred_element_type=jnp.float32).astype(jnp.bfloat16)
    send_grad = jnp.dot(cotangent, placing, preferred_element_type=jnp.float32).astype(jnp.bfloat16)
    recv_in, recv_grad = (
        lax.all_to_all(send_in, "expert", split_axis=1, concat_axis=1, tiled=True),
        lax.all_to_all(send_grad, "expert", split_axis=1, concat_axis=1, tiled=True),
    )
    feature_piece = lax.all_gather(recv_in, "tensor", axis=0, tiled=True)
    grad_piece = lax.all_gather(recv_grad, "tensor", axis=0, tiled=True)
    gate_rows = gate_local
    up_rows = up_local
    gate_sum = lax.dot_general(
        feature_piece, gate_rows, first_dims, preferred_element_type=jnp.float32
    )
    up_sum = lax.dot_general(feature_piece, up_rows, first_dims, preferred_element_type=jnp.float32)
    hidden_grad = lax.dot_general(
        grad_piece, down_local, down_dims, preferred_element_type=jnp.float32
    )
    gate_sum, up_sum, hidden_grad = (gate_sum, up_sum, hidden_grad)
    grad_gate, grad_up, score_rows = swiglu_backward(gate_sum, up_sum, hidden_grad)
    gate_rows = gate_local
    up_rows = up_local
    term = lax.dot_general(gate_rows, grad_gate, hidden_dims, preferred_element_type=jnp.float32)
    term = term + lax.dot_general(up_rows, grad_up, hidden_dims, preferred_element_type=jnp.float32)
    tensor_count = lax.axis_size("tensor")
    score_high = score_rows.astype(jnp.bfloat16)
    score_low = (score_rows - score_high.astype(jnp.float32)).astype(jnp.bfloat16)
    extra = jnp.concatenate(
        [
            score_high[None, :],
            score_low[None, :],
            jnp.zeros((EXTRA_ROWS - 2, slot_total), jnp.bfloat16),
        ],
        axis=0,
    )
    blocks = term.astype(jnp.bfloat16).reshape(tensor_count, features_here, slot_total)
    extra = jnp.broadcast_to(extra[None], (tensor_count, EXTRA_ROWS, slot_total))
    parts = lax.all_to_all(
        jnp.concatenate([blocks, extra], axis=1), "tensor", split_axis=0, concat_axis=0, tiled=True
    ).astype(jnp.float32)
    totals = jnp.sum(parts, axis=0)
    score = (
        totals[features_here : features_here + 1] + totals[features_here + 1 : features_here + 2]
    )
    score_high = score.astype(jnp.bfloat16)
    score_low = (score - score_high.astype(jnp.float32)).astype(jnp.bfloat16)
    summed = jnp.concatenate(
        [
            totals[:features_here].astype(jnp.bfloat16),
            score_high,
            score_low,
            jnp.zeros((EXTRA_ROWS - 2, slot_total), jnp.bfloat16),
        ],
        axis=0,
    )
    back = lax.all_to_all(summed, "expert", split_axis=1, concat_axis=1, tiled=True)
    back = back.astype(jnp.float32)
    back_terms = back[:features_here]
    back_scores = (
        back[features_here : features_here + 1] + back[features_here + 1 : features_here + 2]
    )
    grad_local = jnp.dot(
        back_terms, weighting.T, precision=lax.Precision.HIGHEST, preferred_element_type=jnp.float32
    )
    score_grad = jnp.sum(
        jnp.where(matches, back_scores[0][None, None, :], jnp.float32(0.0)), axis=2
    )
    grad_input = grad_local.astype(jnp.bfloat16)
    return (grad_input, score_grad)


def solution(mesh):
    in_specs = (
        P("tensor", "expert"),
        P("tensor", "expert"),
        P("expert", None),
        P("expert", None),
        P("expert", None, "tensor"),
        P("expert", None, "tensor"),
        P("expert", "tensor", None),
    )
    out_specs = (P("tensor", "expert"), P("expert", None))
    return jax.shard_map(body, mesh=mesh, in_specs=in_specs, out_specs=out_specs, check_vma=False)
```

profile of v0, /device:TPU:0, one launch (start us, length us, event | category | flops | bytes accessed | tf_op | source)
XLA Modules:
  0.0 178.5 jit_solution(15263084820237573660)
XLA Ops:
  7.2 0.0 copy-start
  7.2 0.0 all-gather.5.cloned.1.call-start
  7.2 0.7 convert_reduce_fusion.2
  7.9 0.1 fusion.23
  8.1 0.7 select_reduce_fusion.2
  8.8 0.7 convert_add_fusion
  9.5 0.0 copy-done
  9.5 0.2 convolution_convert_fusion
  9.8 14.7 %all_to_all.38 = bf16[384,4,80]{0,2,1:T(8,128)(2,1)} all-to-all(bf16[384,4,80]{0,2,1:T(8,128)(2,1)S(1)} %bitcast.50), channel_id=1, replica_groups=mesh['expert'=4,'tensor'=8] {'expert'}, dimensions={1} | all-to-all | bytes 491520 | tf_op jit(solution)/shard_map/all_to_all | solution.py:51
  24.5 0.0 all-gather.5.cloned.1.call-update
  24.5 0.0 all-gather.3.cloned.1.call-start
  24.6 1.1 convolution_convert_fusion.1
  25.7 10.7 %all_to_all.39 = bf16[384,4,80]{0,2,1:T(8,128)(2,1)} all-to-all(bf16[384,4,80]{0,2,1:T(8,128)(2,1)S(1)} %bitcast.49), channel_id=1, replica_groups=mesh['expert'=4,'tensor'=8] {'expert'}, dimensions={1} | all-to-all | bytes 491520 | tf_op jit(solution)/shard_map/all_to_all | solution.py:52
  36.5 0.0 all-gather.3.cloned.1.call-update
  36.5 14.9 %all-gather.5.cloned.1.call-done = bf16[3072,320]{0,1:T(8,128)(2,1)} async-done(((bf16[384,320]{0,1:T(8,128)(2,1)}), bf16[3072,320]{0,1:T(8,128)(2,1)}) %all-gather.5.cloned.1.call-update) | async-done | bytes 1966096 | tf_op jit(solution)/shard_map/all_gather | solution.py:54
  51.4 0.0 copy-start.3
  51.4 9.4 %fusion.2 = f32[320,2048]{1,0:T(8,128)S(1)} fusion(bf16[3072,320]{0,1:T(8,128)(2,1)} %all-gather.5.cloned.1.call-done, bf16[1,3072,2048]{2,1,0:T(8,128)(2,1)} %param.11), kind=kOutput, calls=%fused_computation.2 | convolution fusion | flops 4026531840 | bytes 17170432 | tf_op jit(solution)/shard_map/dot_general | solution.py:58
  60.8 0.0 copy-done.3
  60.8 8.8 %fusion.6 = f32[320,2048]{1,0:T(8,128)} fusion(bf16[3072,320]{0,1:T(8,128)(2,1)S(1)} %copy-done.3, bf16[1,3072,2048]{2,1,0:T(8,128)(2,1)} %param.12), kind=kOutput, calls=%fused_computation.6 | convolution fusion | flops 4026531840 | bytes 17170432 | tf_op jit(solution)/shard_map/dot_general | solution.py:61
  69.6 11.3 %all-gather.3.cloned.1.call-done = bf16[3072,320]{0,1:T(8,128)(2,1)} async-done(((bf16[384,320]{0,1:T(8,128)(2,1)}), bf16[3072,320]{0,1:T(8,128)(2,1)}) %all-gather.3.cloned.1.call-update) | async-done | bytes 1966096 | tf_op jit(solution)/shard_map/all_gather | solution.py:55
  80.9 12.0 %multiply_reduce_fusion = (f32[320]{0:T(512)S(1)}, f32[320,2048]{1,0:T(8,128)}) fusion(f32[320,2048]{1,0:T(8,128)} %fusion.6, f32[320,2048]{1,0:T(8,128)S(1)} %fusion.2, bf16[3072,320]{0,1:T(8,128)(2,1)} %all-gather.3.cloned.1.call-done, bf16[1,2048,3072]{2,1,0:T(8,128)(2,1)} %param.13), kind=kOutput, calls=%fused_computation.14 | convolution fusion | flops 4031119104 | bytes 22414592 | tf_op jit(solution)/shard_map/dot_general | solution.py:62
  93.0 12.8 %fusion = f32[320,3072]{1,0:T(8,128)} fusion(bf16[1,3072,2048]{2,1,0:T(8,128)(2,1)} %param.11, f32[320,2048]{1,0:T(8,128)S(1)} %fusion.2, f32[320,2048]{1,0:T(8,128)} %get-tuple-element.7, f32[320,2048]{1,0:T(8,128)} %fusion.6), kind=kOutput, calls=%fused_computation | convolution fusion | flops 4033085440 | bytes 24379392 | tf_op jit(solution)/shard_map/dot_general | solution.py:69
  105.8 12.1 %fusion.16 = bf16[3072,320]{0,1:T(8,128)(2,1)} fusion(f32[320,3072]{1,0:T(8,128)} %fusion, bf16[1,3072,2048]{2,1,0:T(8,128)(2,1)} %param.12, f32[320,2048]{1,0:T(8,128)} %get-tuple-element.7, f32[320,2048]{1,0:T(8,128)S(1)} %fusion.2), kind=kOutput, calls=%fused_computation.13 | convolution fusion | flops 4032430080 | bytes 23724032 | tf_op jit(solution)/shard_map/dot_general | solution.py:70
  117.9 2.9 %copy.40 = bf16[3072,320]{1,0:T(8,128)(2,1)S(1)} copy(bf16[3072,320]{0,1:T(8,128)(2,1)} %fusion.16) | data formatting | bytes 3932160 | tf_op jit(solution)/shard_map/reshape | solution.py:82
  120.9 0.3 pad_maximum_fusion
  121.1 33.0 %all_to_all.40 = bf16[8,400,320]{2,1,0:T(8,128)(2,1)S(1)} all-to-all(bf16[8,400,320]{2,1,0:T(8,128)(2,1)S(1)} %pad_maximum_fusion), channel_id=1, replica_groups=mesh['expert'=4,'tensor'=8] {'tensor'}, dimensions={0} | all-to-all | bytes 4096000 | tf_op jit(solution)/shard_map/all_to_all | solution.py:84
  154.1 0.0 copy-start.1
  154.1 0.4 convert_reduce_fusion
  154.5 0.0 copy-start.2
  154.7 0.2 copy.39
  154.8 14.5 %all_to_all.41 = bf16[400,4,80]{0,2,1:T(8,128)(2,1)S(1)} all-to-all(bf16[400,4,80]{0,2,1:T(8,128)(2,1)S(1)} %bitcast.45), channel_id=1, replica_groups=mesh['expert'=4,'tensor'=8] {'expert'}, dimensions={1} | all-to-all | bytes 512000 | tf_op jit(solution)/shard_map/all_to_all | solution.py:102
  169.3 0.1 convert_element_type.115
  169.4 0.2 fusion.22
  169.6 0.1 broadcast_in_dim.57
  169.7 0.0 copy-done.2
  169.7 0.7 select_reduce_fusion
  170.4 1.2 convolution_convert_fusion.2
  171.6 0.0 copy-done.1
  (10 shorter events, 0.2 us)
Async XLA Ops:
  7.2 2.3 %copy-start = (bf16[384,128]{1,0:T(8,128)(2,1)S(1)}, bf16[384,128]{1,0:T(8,128)(2,1)}, u32[]{:S(2)}) copy-start(bf16[384,128]{1,0:T(8,128)(2,1)} %param.7) | copy-start | bytes 294916
  7.2 44.2 %all-gather.5.cloned.1.call-start = ((), (), s32[]{:S(2)}) async-start(), calls=%async_computation.5 | async-start | bytes 2211840 | tf_op jit(solution)/shard_map/all_gather | solution.py:54
  24.5 56.4 %all-gather.3.cloned.1.call-start = ((), (), s32[]{:S(2)}) async-start(), calls=%async_computation.4 | async-start | bytes 2211840 | tf_op jit(solution)/shard_map/all_gather | solution.py:55
  51.4 9.4 %copy-start.3 = (bf16[3072,320]{0,1:T(8,128)(2,1)S(1)}, bf16[3072,320]{0,1:T(8,128)(2,1)}, u32[]{:S(2)}) copy-start(bf16[3072,320]{0,1:T(8,128)(2,1)} %all-gather.5.cloned.1.call-done) | copy-start | bytes 5898244
  154.1 17.5 %copy-start.1 = (bf16[384,128]{1,0:T(8,128)(2,1)S(1)}, bf16[384,128]{1,0:T(8,128)(2,1)}, u32[]{:S(2)}) copy-start(bf16[384,128]{1,0:T(8,128)(2,1)} %param.7) | copy-start | bytes 294916
  154.5 15.2 %copy-start.2 = (f32[128,2]{0,1:T(2,128)S(1)}, f32[128,2]{0,1:T(2,128)}, u32[]{:S(2)}) copy-start(f32[128,2]{0,1:T(2,128)} %param.10) | copy-start | bytes 3076
Sparse Core Ops, SparseCore 0:
  24.7 26.7 all-gather.4
  53.3 27.6 all-gather.2
where the time goes:
time: 179 us; the launch traced here: 178 us
  blocking collectives  73 us (41%)
  matrix products  57.8 us (32%)
  waiting for transfers between devices  26.3 us (15%)
  between operations  14.2 us (8%)
  other arithmetic  3.87 us (2%)
  local copies, waits for them, and re-layouts  3.26 us (2%)
    all_to_all x1, blocking collectives, body(): lax.all_to_all(jnp.concatenate([blocks, extra], axis=1), 'tensor', split_...  33 us
    all_gather x1, waiting for transfers between devices, body(): feature_piece = lax.all_gather(recv_in, 'tensor', axis=0, tiled=True)  14.9 us
    all_to_all x1, blocking collectives, body(): lax.all_to_all(send_in, 'expert', split_axis=1, concat_axis=1, tiled=True)  14.7 us
    all_to_all x1, blocking collectives, body(): lax.all_to_all(summed, 'expert', split_axis=1, concat_axis=1, tiled=True)  14.5 us
    dot_general x1, matrix products, body(): lax.dot_general(gate_rows, grad_gate, hidden_dims, preferred_element_type...  12.8 us
    dot_general x1, matrix products, body(): lax.dot_general(up_rows, grad_up, hidden_dims, preferred_element_type=jnp...  12.1 us
    dot_general x1, matrix products, body(): lax.dot_general(grad_piece, down_local, down_dims, preferred_element_type...  12 us
    all_gather x1, waiting for transfers between devices, body(): grad_piece = lax.all_gather(recv_grad, 'tensor', axis=0, tiled=True)  11.3 us
  transfers between devices with their start and end apart: 2, of which 2 were waited for; matrix products, arithmetic and copies ran while one was open for 11% of the time, Pallas kernels for 0%

commit v1 on v0

--- a/solution.py
+++ b/solution.py
@@ -4,6 +4,22 @@
 from jax.sharding import PartitionSpec as P
 
 EXTRA_ROWS = 16
+
+
+def exchange_in_pairs(x, axis, split, join):
+    ways, here = (lax.axis_size(axis), lax.axis_index(axis))
+    width = x.shape[split] // ways
+    dims = list(x.shape)
+    dims[split] = width
+    height = dims[join]
+    dims[join] = height * ways
+    full = jnp.zeros(dims, x.dtype)
+    for mask in range(ways):
+        part = lax.dynamic_slice_in_dim(x, (here ^ mask) * width, width, axis=split)
+        if mask:
+            part = lax.ppermute(part, axis, [(d, d ^ mask) for d in range(ways)])
+        full = lax.dynamic_update_slice_in_dim(full, part, (here ^ mask) * height, axis=join)
+    return full
 
 
 def slot_numbers(route_ids, expert_count, capacity):
@@ -49,7 +65,7 @@
     send_grad = jnp.dot(cotangent, placing, preferred_element_type=jnp.float32).astype(jnp.bfloat16)
     recv_in, recv_grad = (
         lax.all_to_all(send_in, "expert", split_axis=1, concat_axis=1, tiled=True),
-        lax.all_to_all(send_grad, "expert", split_axis=1, concat_axis=1, tiled=True),
+        exchange_in_pairs(send_grad, "expert", 1, 1),
     )
     feature_piece = lax.all_gather(recv_in, "tensor", axis=0, tiled=True)
     grad_piece = lax.all_gather(recv_grad, "tensor", axis=0, tiled=True)

time: 179 us -> 179 us (level)
  blocking collectives: 73 us -> 62.2 us
  waiting for transfers between devices: 26.3 us -> 31.7 us
  starting transfers between devices: 0.08 us -> 4.53 us
    all_to_all x1 -> x0, blocking collectives: 10.7 us -> none  [body(): lax.all_to_all(send_grad, 'expert', split_axis=1, concat_axis=1, tiled=True)]
    ppermute x0 -> x3, starting transfers between devices: none -> 4.45 us  [exchange_in_pairs(): part = lax.ppermute(part, axis, [(d, d ^ mask) for d in range(ways)])]
    ppermute x0 -> x3, waiting for transfers between devices: none -> 3.55 us  [exchange_in_pairs(): part = lax.ppermute(part, axis, [(d, d ^ mask) for d in range(ways)])]
    all_gather x1, waiting for transfers between devices: 14.9 us -> 16.8 us  [body(): feature_piece = lax.all_gather(recv_in, 'tensor', axis=0, tiled=True)]
  transfers between devices with their start and end apart: 2 -> 5, of which waited for: 2 -> 4; matrix products, arithmetic and copies ran while one was open for 11% -> 11% of each run, Pallas kernels for 0% -> 0%
where the time goes in v1:
time: 179 us; the launch traced here: 178 us
  blocking collectives  62.2 us (35%)
  matrix products  57.8 us (32%)
  waiting for transfers between devices  31.7 us (18%)
  between operations  14.2 us (8%)
  starting transfers between devices  4.53 us (3%)
  local copies, waits for them, and re-layouts  4.08 us (2%)
  other arithmetic  3.87 us (2%)
    all_to_all x1, blocking collectives, body(): lax.all_to_all(jnp.concatenate([blocks, extra], axis=1), 'tensor', split_...  33 us
    all_gather x1, waiting for transfers between devices, body(): feature_piece = lax.all_gather(recv_in, 'tensor', axis=0, tiled=True)  16.8 us
    all_to_all x1, blocking collectives, body(): lax.all_to_all(send_in, 'expert', split_axis=1, concat_axis=1, tiled=True)  14.7 us
    all_to_all x1, blocking collectives, body(): lax.all_to_all(summed, 'expert', split_axis=1, concat_axis=1, tiled=True)  14.5 us
    dot_general x1, matrix products, body(): lax.dot_general(gate_rows, grad_gate, hidden_dims, preferred_element_type...  12.8 us
    dot_general x1, matrix products, body(): lax.dot_general(up_rows, grad_up, hidden_dims, preferred_element_type=jnp...  12.1 us
    dot_general x1, matrix products, body(): lax.dot_general(grad_piece, down_local, down_dims, preferred_element_type...  12 us
    all_gather x1, waiting for transfers between devices, body(): grad_piece = lax.all_gather(recv_grad, 'tensor', axis=0, tiled=True)  11.3 us
  transfers between devices with their start and end apart: 5, of which 4 were waited for; matrix products, arithmetic and copies ran while one was open for 11% of the time, Pallas kernels for 0%

profile of v1, /device:TPU:0, one launch (start us, length us, event | category | flops | bytes accessed | tf_op | source)
XLA Modules:
  0.0 178.5 jit_solution(17193575185479264435)
XLA Ops:
  7.2 0.0 copy-start
  7.2 0.0 all-gather.5.cloned.1.call-start
  7.2 0.7 convert_reduce_fusion.2
  7.9 0.1 fusion.23
  8.1 0.7 select_reduce_fusion.2
  8.8 0.7 convert_add_fusion
  9.5 0.0 copy-done
  9.5 0.2 convolution_convert_fusion
  9.8 14.7 %all_to_all.26 = bf16[384,4,80]{0,2,1:T(8,128)(2,1)} all-to-all(bf16[384,4,80]{0,2,1:T(8,128)(2,1)S(1)} %bitcast.52), channel_id=1, replica_groups=mesh['expert'=4,'tensor'=8] {'expert'}, dimensions={1} | all-to-all | bytes 491520 | tf_op jit(solution)/shard_map/all_to_all | solution.py:67
  24.5 0.0 all-gather.5.cloned.1.call-update
  24.5 0.0 all-gather.3.cloned.1.call-start
  24.6 1.1 convolution_convert_fusion.1
  25.8 0.3 collective-permute-start
  26.1 1.8 collective-permute-start.1
  27.9 2.4 %collective-permute-start.2 = (bf16[384,80]{0,1:T(8,128)(2,1)S(1)}, bf16[384,80]{0,1:T(8,128)(2,1)S(1)}, u32[]{:S(2)}, u32[]{:S(2)}) collective-permute-start(bf16[384,80]{0,1:T(8,128)(2,1)S(1)} %get-tuple-element.6), channel_id=1, source_target_pairs={{0,24},{8,16},{16,8},{24,0},{1,25},{9,17},{17,9},{25,1},{2,26},{10... | collective-permute-start | bytes 184328 | tf_op jit(solution)/shard_map/ppermute | solution.py:20
  30.3 0.0 collective-permute-done
  30.3 2.2 %collective-permute-done.1 = bf16[384,80]{0,1:T(8,128)(2,1)S(1)} collective-permute-done((bf16[384,80]{0,1:T(8,128)(2,1)S(1)}, bf16[384,80]{0,1:T(8,128)(2,1)S(1)}, u32[]{:S(2)}, u32[]{:S(2)}) %collective-permute-start.1) | collective-permute-done | bytes 61472 | tf_op jit(solution)/shard_map/ppermute | solution.py:20
  32.6 1.3 collective-permute-done.2
  33.9 0.0 copy-start.2
  33.9 0.7 copy-done.2
  34.6 0.0 all-gather.3.cloned.1.call-update
  34.6 16.8 %all-gather.5.cloned.1.call-done = bf16[3072,320]{0,1:T(8,128)(2,1)} async-done(((bf16[384,320]{0,1:T(8,128)(2,1)}), bf16[3072,320]{0,1:T(8,128)(2,1)}) %all-gather.5.cloned.1.call-update) | async-done | bytes 1966096 | tf_op jit(solution)/shard_map/all_gather | solution.py:70
  51.4 0.0 copy-start.4
  51.4 9.4 %fusion.2 = f32[320,2048]{1,0:T(8,128)S(1)} fusion(bf16[3072,320]{0,1:T(8,128)(2,1)} %all-gather.5.cloned.1.call-done, bf16[1,3072,2048]{2,1,0:T(8,128)(2,1)} %param.11), kind=kOutput, calls=%fused_computation.2 | convolution fusion | flops 4026531840 | bytes 17170432 | tf_op jit(solution)/shard_map/dot_general | solution.py:74
  60.8 0.0 copy-done.4
  60.8 8.8 %fusion.6 = f32[320,2048]{1,0:T(8,128)} fusion(bf16[3072,320]{0,1:T(8,128)(2,1)S(1)} %copy-done.4, bf16[1,3072,2048]{2,1,0:T(8,128)(2,1)} %param.12), kind=kOutput, calls=%fused_computation.6 | convolution fusion | flops 4026531840 | bytes 17170432 | tf_op jit(solution)/shard_map/dot_general | solution.py:77
  69.6 11.3 %all-gather.3.cloned.1.call-done = bf16[3072,320]{0,1:T(8,128)(2,1)} async-done(((bf16[384,320]{0,1:T(8,128)(2,1)}), bf16[3072,320]{0,1:T(8,128)(2,1)}) %all-gather.3.cloned.1.call-update) | async-done | bytes 1966096 | tf_op jit(solution)/shard_map/all_gather | solution.py:71
  80.9 12.0 %multiply_reduce_fusion = (f32[320]{0:T(512)S(1)}, f32[320,2048]{1,0:T(8,128)}) fusion(f32[320,2048]{1,0:T(8,128)} %fusion.6, f32[320,2048]{1,0:T(8,128)S(1)} %fusion.2, bf16[3072,320]{0,1:T(8,128)(2,1)} %all-gather.3.cloned.1.call-done, bf16[1,2048,3072]{2,1,0:T(8,128)(2,1)} %param.13), kind=kOutput, calls=%fused_computation.14 | convolution fusion | flops 4031119104 | bytes 22414592 | tf_op jit(solution)/shard_map/dot_general | solution.py:78
  93.0 12.8 %fusion = f32[320,3072]{1,0:T(8,128)} fusion(bf16[1,3072,2048]{2,1,0:T(8,128)(2,1)} %param.11, f32[320,2048]{1,0:T(8,128)S(1)} %fusion.2, f32[320,2048]{1,0:T(8,128)} %get-tuple-element.10, f32[320,2048]{1,0:T(8,128)} %fusion.6), kind=kOutput, calls=%fused_computation | convolution fusion | flops 4033085440 | bytes 24379392 | tf_op jit(solution)/shard_map/dot_general | solution.py:85
  105.8 12.1 %fusion.16 = bf16[3072,320]{0,1:T(8,128)(2,1)} fusion(f32[320,3072]{1,0:T(8,128)} %fusion, bf16[1,3072,2048]{2,1,0:T(8,128)(2,1)} %param.12, f32[320,2048]{1,0:T(8,128)} %get-tuple-element.10, f32[320,2048]{1,0:T(8,128)S(1)} %fusion.2), kind=kOutput, calls=%fused_computation.13 | convolution fusion | flops 4032430080 | bytes 23724032 | tf_op jit(solution)/shard_map/dot_general | solution.py:86
  117.9 2.9 %copy.40 = bf16[3072,320]{1,0:T(8,128)(2,1)S(1)} copy(bf16[3072,320]{0,1:T(8,128)(2,1)} %fusion.16) | data formatting | bytes 3932160 | tf_op jit(solution)/shard_map/reshape | solution.py:98
  120.9 0.3 pad_maximum_fusion
  121.1 33.0 %all_to_all.27 = bf16[8,400,320]{2,1,0:T(8,128)(2,1)S(1)} all-to-all(bf16[8,400,320]{2,1,0:T(8,128)(2,1)S(1)} %pad_maximum_fusion), channel_id=1, replica_groups=mesh['expert'=4,'tensor'=8] {'tensor'}, dimensions={0} | all-to-all | bytes 4096000 | tf_op jit(solution)/shard_map/all_to_all | solution.py:100
  154.1 0.0 copy-start.1
  154.1 0.4 convert_reduce_fusion
  154.5 0.0 copy-start.3
  154.7 0.2 copy.39
  154.8 14.5 %all_to_all.28 = bf16[400,4,80]{0,2,1:T(8,128)(2,1)S(1)} all-to-all(bf16[400,4,80]{0,2,1:T(8,128)(2,1)S(1)} %bitcast.49), channel_id=1, replica_groups=mesh['expert'=4,'tensor'=8] {'expert'}, dimensions={1} | all-to-all | bytes 512000 | tf_op jit(solution)/shard_map/all_to_all | solution.py:118
  169.3 0.1 convert_element_type.112
  169.4 0.2 fusion.22
  169.6 0.1 broadcast_in_dim.61
  169.7 0.0 copy-done.3
  169.7 0.7 select_reduce_fusion
  170.4 1.2 convolution_convert_fusion.2
  171.6 0.0 copy-done.1
  (16 shorter events, 0.3 us)
Async XLA Ops:
  7.2 2.3 %copy-start = (bf16[384,128]{1,0:T(8,128)(2,1)S(1)}, bf16[384,128]{1,0:T(8,128)(2,1)}, u32[]{:S(2)}) copy-start(bf16[384,128]{1,0:T(8,128)(2,1)} %param.7) | copy-start | bytes 294916
  7.2 44.2 %all-gather.5.cloned.1.call-start = ((), (), s32[]{:S(2)}) async-start(), calls=%async_computation.4 | async-start | bytes 2211840 | tf_op jit(solution)/shard_map/all_gather | solution.py:70
  24.5 56.4 %all-gather.3.cloned.1.call-start = ((), (), s32[]{:S(2)}) async-start(), calls=%async_computation.3 | async-start | bytes 2211840 | tf_op jit(solution)/shard_map/all_gather | solution.py:71
  25.8 4.5 %collective-permute-start = (bf16[384,80]{0,1:T(8,128)(2,1)S(1)}, bf16[384,80]{0,1:T(8,128)(2,1)S(1)}, u32[]{:S(2)}, u32[]{:S(2)}) collective-permute-start(bf16[384,80]{0,1:T(8,128)(2,1)S(1)} %get-tuple-element.8), channel_id=1, source_target_pairs={{0,8},{8,0},{16,24},{24,16},{1,9},{9,1},{17,25},{25,17},{2,10},{10... | collective-permute-start | bytes 184328 | tf_op jit(solution)/shard_map/ppermute | solution.py:20
  26.1 6.4 %collective-permute-start.1 = (bf16[384,80]{0,1:T(8,128)(2,1)S(1)}, bf16[384,80]{0,1:T(8,128)(2,1)S(1)}, u32[]{:S(2)}, u32[]{:S(2)}) collective-permute-start(bf16[384,80]{0,1:T(8,128)(2,1)S(1)} %get-tuple-element.7), channel_id=1, source_target_pairs={{0,16},{8,24},{16,0},{24,8},{1,17},{9,25},{17,1},{25,9},{2,18},{10... | collective-permute-start | bytes 184328 | tf_op jit(solution)/shard_map/ppermute | solution.py:20
  27.9 6.0 %collective-permute-start.2 = (bf16[384,80]{0,1:T(8,128)(2,1)S(1)}, bf16[384,80]{0,1:T(8,128)(2,1)S(1)}, u32[]{:S(2)}, u32[]{:S(2)}) collective-permute-start(bf16[384,80]{0,1:T(8,128)(2,1)S(1)} %get-tuple-element.6), channel_id=1, source_target_pairs={{0,24},{8,16},{16,8},{24,0},{1,25},{9,17},{17,9},{25,1},{2,26},{10... | collective-permute-start | bytes 184328 | tf_op jit(solution)/shard_map/ppermute | solution.py:20
  33.9 0.7 copy-start.2
  51.4 9.4 %copy-start.4 = (bf16[3072,320]{0,1:T(8,128)(2,1)S(1)}, bf16[3072,320]{0,1:T(8,128)(2,1)}, u32[]{:S(2)}) copy-start(bf16[3072,320]{0,1:T(8,128)(2,1)} %all-gather.5.cloned.1.call-done) | copy-start | bytes 5898244
  154.1 17.5 %copy-start.1 = (bf16[384,128]{1,0:T(8,128)(2,1)S(1)}, bf16[384,128]{1,0:T(8,128)(2,1)}, u32[]{:S(2)}) copy-start(bf16[384,128]{1,0:T(8,128)(2,1)} %param.7) | copy-start | bytes 294916
  154.5 15.2 %copy-start.3 = (f32[128,2]{0,1:T(2,128)S(1)}, f32[128,2]{0,1:T(2,128)}, u32[]{:S(2)}) copy-start(f32[128,2]{0,1:T(2,128)} %param.10) | copy-start | bytes 3076
Sparse Core Ops, SparseCore 0:
  24.7 26.7 all-gather.4
  53.3 27.6 all-gather.2
